TPU v7x, 128 devices: a whole 4x4x4 slice. The times are simulated.
128 devices in a mesh: grp: 8 (over x, core), grid: 16 (over z, y).
Axes of the slice: x: 4, y: 4, z: 4, core: 2. Of those that a mesh axis runs over, the one named last changes fastest.
Arguments:
- dy_quant: bfloat16 [8, 8, 256, 8192], P(None, 'grp', 'grid'), may hold values from -4 to 4
- dy_scale: bfloat16 [8, 8, 256, 64], P(None, 'grp', 'grid'), may hold values from 0.049804688 to 1
- tokens: bfloat16 [8, 8, 256, 5120], P(None, 'grp', 'grid'), may hold values from -1.1953125 to 1.1953125
- weight: bfloat16 [8, 16, 1280, 2048], P('grp', 'grid'), may hold values from -0.078125 to 0.078125
- counts: int32 [8, 8], replicated, may hold values from 1 to 256, as said below
Outputs:
- dx_quant: bfloat16 [8, 8, 256, 5120], P(None, 'grp', 'grid')
- dx_scale: bfloat16 [8, 8, 256, 40], P(None, 'grp', 'grid')
- dw_quant: bfloat16 [8, 16, 1280, 2048], P('grp', 'grid')
- dw_scale: float32 [8, 16, 10, 16], P('grp', 'grid')
Inputs may be any that keep to these rules, and one draw needn't show every extreme that they name: `counts`: some replica fills all 256 slots of some expert; the other slots of a row are padding.
All inputs are finite; a program needn't handle non-finite values. Where the computation divides by a largest or mean magnitude, that divisor is 1e-20 or more.
Results may differ from a plain program's by a relative error of at most 0.0051.
Values may be sent and summed in bfloat16 or wider, within the bound.
A program may use at most 192 MiB of HBM per device.

v0:
```python
import jax
import jax.numpy as jnp
from jax import lax
from jax.sharding import PartitionSpec as P

QB = 128
GC = 4


EPS = 1e-06


def fan_out(values, row_blocks, col_blocks, by_column):
    lead = values.shape[:-2]
    rows = values.shape[-2]
    width = values.shape[-1]
    parts = col_blocks if by_column else row_blocks
    piece = width // parts
    split = jnp.moveaxis(values.reshape(lead + (rows, parts, piece)), -2, -3)
    if by_column:
        wide = jnp.broadcast_to(
            split[..., None, :, :, :], lead + (row_blocks, col_blocks, rows, piece)
        )
    else:
        wide = jnp.broadcast_to(
            split[..., :, None, :, :], lead + (row_blocks, col_blocks, rows, piece)
        )
    return wide.reshape(lead + (row_blocks * col_blocks, rows, piece))


def dequantize(quantized, scales, live):
    replicas, rows, hidden = quantized.shape
    col_groups = scales.shape[-1]
    values = quantized.astype(jnp.float32).reshape(replicas, rows, col_groups, hidden // col_groups)
    values = values * scales.astype(jnp.float32)[..., None]
    return jnp.where(live[:, :, None], values.reshape(replicas, rows, hidden), 0.0).astype(
        jnp.bfloat16
    )


def on_device(dy_quant, dy_scale, tokens, weight, counts):
    group = lax.axis_index("grp")
    tiles = lax.axis_size("grid")
    row_blocks = tiles // GC
    quant_in, scale_in, token_in = (
        lax.all_to_all(dy_quant, "grp", split_axis=0, concat_axis=1, tiled=True),
        lax.all_to_all(dy_scale, "grp", split_axis=0, concat_axis=1, tiled=True),
        lax.all_to_all(tokens, "grp", split_axis=0, concat_axis=1, tiled=True),
    )
    quant_got, scale_got, token_got = (
        lax.all_to_all(
            fan_out(quant_in, row_blocks, GC, True), "grid", split_axis=2, concat_axis=2, tiled=True
        ),
        lax.all_to_all(
            fan_out(scale_in, row_blocks, GC, True), "grid", split_axis=2, concat_axis=2, tiled=True
        ),
        lax.all_to_all(
            fan_out(token_in, row_blocks, GC, False),
            "grid",
            split_axis=2,
            concat_axis=2,
            tiled=True,
        ),
    )
    replicas = quant_got.shape[1]
    shard = quant_got.shape[3]
    slots = tiles * shard
    quant_rows = quant_got[0].reshape(replicas, slots, quant_got.shape[-1])
    scale_rows = scale_got[0].reshape(replicas, slots, scale_got.shape[-1])
    token_rows = token_got[0].reshape(replicas, slots, token_got.shape[-1])
    weight_tile = weight[0, 0]
    height = weight_tile.shape[0]
    breadth = weight_tile.shape[1]
    live_count = lax.dynamic_slice_in_dim(counts, group, 1, 1)[:, 0]
    anchor = jnp.zeros((), jnp.int32)
    factor = 1
    for level in range(8):
        if factor * 2 * shard * replicas <= 512 and slots % (factor * 2 * shard) == 0:
            factor = factor * 2
    block = factor * shard

    def compute(start, state):
        sum_weight, sum_input = state
        positions = start + jnp.arange(block, dtype=jnp.int32)
        live = positions[None, :] < live_count[:, None]
        quantized = lax.dynamic_slice_in_dim(quant_rows, start, block, 1)
        scales = lax.dynamic_slice_in_dim(scale_rows, start, block, 1)
        gradient = dequantize(quantized, scales, live)
        part_input = jnp.einsum(
            "rkf,df->rkd", gradient, weight_tile, preferred_element_type=jnp.float32
        )
        sum_input = lax.dynamic_update_slice(sum_input, part_input, (anchor, start, anchor))
        inputs = lax.dynamic_slice_in_dim(token_rows, start, block, 1)
        sum_weight = sum_weight + jnp.einsum(
            "rkd,rkf->df", inputs, gradient, preferred_element_type=jnp.float32
        )
        return (sum_weight, sum_input)

    def loop_body(counter, carry):
        start = (counter * block).astype(jnp.int32)
        return compute(start, carry)

    initial = (
        jnp.zeros((height, breadth), jnp.float32),
        jnp.zeros((replicas, slots, height), jnp.float32),
    )
    sum_weight, sum_input = lax.fori_loop(0, slots // block, loop_body, initial)
    outgoing = sum_input.reshape(replicas, tiles, shard, height)
    incoming = lax.all_to_all(outgoing, "grid", split_axis=1, concat_axis=1, tiled=True)
    summed = jnp.sum(incoming.reshape(replicas, row_blocks, GC, shard, height), axis=2)
    grad_input = jnp.moveaxis(summed, 1, 2).reshape(replicas, shard, row_blocks * height)
    width = row_blocks * height
    groups_x = grad_input.reshape(replicas, shard, width // QB, QB)
    scale_x = jnp.max(jnp.abs(groups_x), axis=3) + EPS
    quantized_x = (
        (groups_x / scale_x[..., None]).reshape(replicas, shard, width).astype(jnp.bfloat16)
    )
    out_input, out_scale = (
        lax.all_to_all(quantized_x[None], "grp", split_axis=1, concat_axis=0, tiled=True),
        lax.all_to_all(
            scale_x.astype(jnp.bfloat16)[None], "grp", split_axis=1, concat_axis=0, tiled=True
        ),
    )
    blocks_w = sum_weight.reshape(height // QB, QB, breadth // QB, QB)
    scale_w = jnp.max(jnp.abs(blocks_w), axis=(1, 3)) + EPS
    quantized_w = (
        (blocks_w / scale_w[:, None, :, None]).reshape(height, breadth).astype(jnp.bfloat16)
    )
    return (out_input, out_scale, quantized_w[None, None], scale_w[None, None])


def solution(mesh):
    return jax.shard_map(
        on_device,
        mesh=mesh,
        in_specs=(
            P(None, "grp", "grid", None),
            P(None, "grp", "grid", None),
            P(None, "grp", "grid", None),
            P("grp", "grid", None, None),
            P(),
        ),
        out_specs=(
            P(None, "grp", "grid", None),
            P(None, "grp", "grid", None),
            P("grp", "grid", None, None),
            P("grp", "grid", None, None),
        ),
        check_vma=False,
    )
```

profile of v0, /device:TPU:1, one launch (start us, length us, event | category | flops | bytes accessed | tf_op | source)
XLA Modules:
  0.0 635.1 jit_solution(353473075076525728)
XLA Ops:
  0.6 0.9 reshape.175
  1.5 10.2 %all_to_all.71 = bf16[8,2,512]{2,1,0:T(2,128)(2,1)S(1)} all-to-all(bf16[8,2,512]{2,1,0:T(2,128)(2,1)S(1)} %reshape.175), channel_id=1, replica_groups=mesh['grp'=8,'grid'=16] {'grp'}, dimensions={0} | all-to-all | bytes 32768 | tf_op jit(solution)/shard_map/all_to_all | solution.py:47
  12.7 14.1 %all_to_all.72 = bf16[16,2,1024]{2,1,0:T(2,128)(2,1)S(1)} all-to-all(bf16[16,2,1024]{2,1,0:T(2,128)(2,1)S(1)} %reshape.177), channel_id=1, replica_groups=mesh['grp'=8,'grid'=16] {'grid'}, dimensions={0} | all-to-all | bytes 131072 | tf_op jit(solution)/shard_map/all_to_all | solution.py:54
  26.8 23.5 %all_to_all.73 = bf16[8,1,16,5120]{3,2,1,0:T(8,128)(2,1)S(1)} all-to-all(bf16[8,1,16,5120]{3,2,1,0:T(8,128)(2,1)} %param.9), channel_id=1, replica_groups=mesh['grp'=8,'grid'=16] {'grp'}, dimensions={0} | all-to-all | bytes 2621440 | tf_op jit(solution)/shard_map/all_to_all | solution.py:48
  50.3 4.5 all-to-all-start.2
  54.8 1.8 reshape.167
  56.7 1.5 copy.20
  58.1 23.1 %all-to-all-done.2 = bf16[8,1,16,8192]{3,2,1,0:T(8,128)(2,1)S(1)} async-done(((bf16[8,1,16,8192]{3,2,1,0:T(8,128)(2,1)}), bf16[8,1,16,8192]{3,2,1,0:T(8,128)(2,1)S(1)}, u32[]{:S(2)}, u32[]{:S(2)}) %all-to-all-start.2) | async-done | bytes 2097184 | tf_op jit(solution)/shard_map/all_to_all | solution.py:46
  81.2 2.9 broadcast_in_dim.82
  84.0 4.6 all-to-all-start.1
  88.7 2.8 reshape.168
  91.4 2.7 copy.23
  94.2 71.9 %all-to-all-done.1 = bf16[1,8,16,16,1280]{4,3,1,0,2:T(8,128)(2,1)} async-done(((bf16[1,8,16,16,1280]{4,3,1,0,2:T(8,128)(2,1)}), bf16[1,8,16,16,1280]{4,3,1,0,2:T(8,128)(2,1)}, u32[]{:S(2)}, u32[]{:S(2)}) %all-to-all-start.1) | async-done | bytes 5242912 | tf_op jit(solution)/shard_map/all_to_all | solution.py:57
  166.0 4.4 broadcast_in_dim.85
  170.4 5.2 all-to-all-start.3
  176.2 5.3 copy.21
  181.5 115.2 %all-to-all-done.3 = bf16[1,8,16,16,2048]{4,3,1,0,2:T(8,128)(2,1)} async-done(((bf16[1,8,16,16,2048]{4,3,1,0,2:T(8,128)(2,1)}), bf16[1,8,16,16,2048]{4,3,1,0,2:T(8,128)(2,1)}, u32[]{:S(2)}, u32[]{:S(2)}) %all-to-all-start.3) | async-done | bytes 8388640 | tf_op jit(solution)/shard_map/all_to_all | solution.py:51
  296.7 8.4 %copy.24 = bf16[1,8,16,16,2048]{4,3,2,1,0:T(8,128)(2,1)} copy(bf16[1,8,16,16,2048]{4,3,1,0,2:T(8,128)(2,1)} %all-to-all-done.3) | data formatting | bytes 16777216 | tf_op jit(solution)/shard_map/all_to_all | solution.py:51
  305.1 4.8 broadcast_in_dim.80
  309.9 94.7 %while.16 = (s32[]{:T(128)}, f32[1280,2048]{1,0:T(8,128)}, f32[8,256,1280]{2,1,0:T(8,128)}, bf16[8,256,1280]{2,1,0:T(8,128)(2,1)}, s32[8,1]{0,1:T(1,128)S(1)}, /...) while((s32[]{:T(128)}, f32[1280,2048]{1,0:T(8,128)}, ...), condition=%wide.region_1.2_spmd.clone, body=%wide.region_0.1_spmd.clone.sunk | while | flops 5378155008 | bytes 71124760 | solution.py:107
  310.0 2.6 mul.39
  312.6 4.9 mul.40
  317.5 3.5 select_convert_fusion.2
  321.0 7.0 %bitcast_add_fusion.2 = f32[1280,2048]{1,0:T(8,128)} fusion(f32[1280,2048]{1,0:T(8,128)} %get-tuple-element.269, bf16[8,64,2048]{2,1,0:T(8,128)(2,1)S(1)} %select_convert_fusion.2, pred[]{:T(512)S(6)} %compare.3, bf16[8,256,1280]{2,1,0:T(8,128)(2,1)} %get-tuple-element.283, s32[]{:T(128)S(6)} %select_n.28), kind=kOutput, calls=%fused_computation.clone.1 | convolution fusion | flops 2689597440 | bytes 24379396 | tf_op jit(solution)/shard_map/while/body/eval_jaxpr/rkd,rkf->df/dot_general | solution.py:94
  328.0 4.5 fusion.22
  332.6 2.6 mul.39
  335.2 4.9 mul.40
  340.0 3.5 select_convert_fusion.2
  343.6 8.5 %bitcast_add_fusion.2 = f32[1280,2048]{1,0:T(8,128)} fusion(f32[1280,2048]{1,0:T(8,128)} %get-tuple-element.269, bf16[8,64,2048]{2,1,0:T(8,128)(2,1)S(1)} %select_convert_fusion.2, pred[]{:T(512)S(6)} %compare.3, bf16[8,256,1280]{2,1,0:T(8,128)(2,1)} %get-tuple-element.283, s32[]{:T(128)S(6)} %select_n.28), kind=kOutput, calls=%fused_computation.clone.1 | convolution fusion | flops 2689597440 | bytes 24379396 | tf_op jit(solution)/shard_map/while/body/eval_jaxpr/rkd,rkf->df/dot_general | solution.py:94
  352.1 4.4 fusion.22
  356.6 2.6 mul.39
  359.2 4.9 mul.40
  364.1 3.5 select_convert_fusion.2
  367.6 8.5 %bitcast_add_fusion.2 = f32[1280,2048]{1,0:T(8,128)} fusion(f32[1280,2048]{1,0:T(8,128)} %get-tuple-element.269, bf16[8,64,2048]{2,1,0:T(8,128)(2,1)S(1)} %select_convert_fusion.2, pred[]{:T(512)S(6)} %compare.3, bf16[8,256,1280]{2,1,0:T(8,128)(2,1)} %get-tuple-element.283, s32[]{:T(128)S(6)} %select_n.28), kind=kOutput, calls=%fused_computation.clone.1 | convolution fusion | flops 2689597440 | bytes 24379396 | tf_op jit(solution)/shard_map/while/body/eval_jaxpr/rkd,rkf->df/dot_general | solution.py:94
  376.1 4.5 fusion.22
  380.7 2.6 mul.39
  383.3 4.9 mul.40
  388.1 3.5 select_convert_fusion.2
  391.7 8.5 %bitcast_add_fusion.2 = f32[1280,2048]{1,0:T(8,128)} fusion(f32[1280,2048]{1,0:T(8,128)} %get-tuple-element.269, bf16[8,64,2048]{2,1,0:T(8,128)(2,1)S(1)} %select_convert_fusion.2, pred[]{:T(512)S(6)} %compare.3, bf16[8,256,1280]{2,1,0:T(8,128)(2,1)} %get-tuple-element.283, s32[]{:T(128)S(6)} %select_n.28), kind=kOutput, calls=%fused_computation.clone.1 | convolution fusion | flops 2689597440 | bytes 24379396 | tf_op jit(solution)/shard_map/while/body/eval_jaxpr/rkd,rkf->df/dot_general | solution.py:94
  400.2 4.5 fusion.22
  404.6 8.8 %copy.28 = f32[8,16,16,1280]{3,2,0,1:T(8,128)} copy(f32[8,16,16,1280]{3,2,1,0:T(8,128)} %bitcast.88) | data formatting | bytes 20971520 | tf_op jit(solution)/shard_map/reshape | solution.py:108
  413.5 5.1 all-to-all-start.6
  418.6 10.2 %abs_bitcast_fusion = f32[160,8,16,128]{3,1,2,0:T(8,128)} fusion(f32[1280,2048]{1,0:T(8,128)} %get-tuple-element.145), kind=kLoop, calls=%fused_computation.14 | loop fusion | flops 2621440 | bytes 20971520
  428.8 6.5 %copy.40 = f32[160,8,16,128]{3,2,1,0:T(8,128)S(1)} copy(f32[160,8,16,128]{3,1,2,0:T(8,128)} %abs_bitcast_fusion) | data formatting | bytes 20971520
  435.3 0.6 bitcast_reduce_fusion
  435.9 132.1 %all-to-all-done.6 = f32[8,16,16,1280]{3,2,0,1:T(8,128)} async-done(((f32[8,16,16,1280]{3,2,0,1:T(8,128)}), f32[8,16,16,1280]{3,2,0,1:T(8,128)}, u32[]{:S(2)}, u32[]{:S(2)}) %all-to-all-start.6) | async-done | bytes 10485792 | tf_op jit(solution)/shard_map/all_to_all | solution.py:109
  568.0 5.4 bitcast_reduce_fusion.1
  573.3 1.8 fusion.9
  575.1 3.2 copy.30
  578.3 3.0 reshape_reshape.3
  581.3 4.9 copy.31
  586.2 4.2 abs.13
  590.4 2.5 reduce_max.18
  592.9 0.7 reshape.179
  593.6 7.3 %all-to-all-start.8 = ((bf16[8,2,320]{2,1,0:T(2,128)(2,1)}), bf16[8,2,320]{2,1,0:T(2,128)(2,1)S(1)}, u32[]{:S(2)}, u32[]{:S(2)}) async-start(bf16[8,2,320]{2,1,0:T(2,128)(2,1)} %reshape.179), calls=%async_computation.8 | async-start | bytes 24576 | tf_op jit(solution)/shard_map/all_to_all | solution.py:120
  600.9 1.9 div.29
  602.8 3.5 div.30
  606.3 3.3 fusion.10
  609.6 4.8 all-to-all-start.7
  614.4 4.6 div.32
  619.0 13.8 %fusion.8 = bf16[1,1,1280,2048]{3,2,1,0:T(8,128)(2,1)} fusion(f32[1280,2048]{1,0:T(8,128)} %get-tuple-element.145, f32[160,8,16,128]{3,2,1,0:T(8,128)} %bitcast.87), kind=kLoop, calls=%fused_computation.15 | loop fusion | flops 5242880 | bytes 26214400 | tf_op jit(solution)/shard_map/broadcast_in_dim | solution.py:129
  632.7 0.6 add.95
  633.4 0.6 bitcast_bitcast_fusion
  634.1 1.1 copy.59
  (51 shorter events, 2.0 us)
Async XLA Ops:
  0.6 175.0 %copy-start = (s32[8,8]{1,0:T(8,128)S(1)}, s32[8,8]{1,0:T(8,128)}, u32[]{:S(2)}) copy-start(s32[8,8]{1,0:T(8,128)} %param.11) | copy-start | bytes 772
  50.3 30.9 %all-to-all-start.2 = ((bf16[8,1,16,8192]{3,2,1,0:T(8,128)(2,1)}), bf16[8,1,16,8192]{3,2,1,0:T(8,128)(2,1)S(1)}, u32[]{:S(2)}, u32[]{:S(2)}) async-start(bf16[8,1,16,8192]{3,2,1,0:T(8,128)(2,1)} %param.7), calls=%async_computation.2 | async-start | bytes 4194304 | tf_op jit(solution)/shard_map/all_to_all | solution.py:46
  84.0 82.0 %all-to-all-start.1 = ((bf16[1,8,16,16,1280]{4,3,1,0,2:T(8,128)(2,1)}), bf16[1,8,16,16,1280]{4,3,1,0,2:T(8,128)(2,1)}, u32[]{:S(2)}, u32[]{:S(2)}) async-start(bf16[1,8,16,16,1280]{4,3,1,0,2:T(8,128)(2,1)} %bitcast.92), calls=%async_computation.1 | async-start | bytes 10485760 | tf_op jit(solution)/shard_map/all_to_all | solution.py:57
  170.4 126.3 %all-to-all-start.3 = ((bf16[1,8,16,16,2048]{4,3,1,0,2:T(8,128)(2,1)}), bf16[1,8,16,16,2048]{4,3,1,0,2:T(8,128)(2,1)}, u32[]{:S(2)}, u32[]{:S(2)}) async-start(bf16[1,8,16,16,2048]{4,3,1,0,2:T(8,128)(2,1)} %bitcast.90), calls=%async_computation.3 | async-start | bytes 16777216 | tf_op jit(solution)/shard_map/all_to_all | solution.py:51
  317.5 10.5 %slice-start = ((s8[5242880]{0:T(1024)(128)(4,1)}), s8[4194304]{0:T(1024)(128)(4,1)S(1)}, s32[]{:S(2)}) async-start(s8[5242880]{0:T(1024)(128)(4,1)} %bitcast.104), calls=%async_computation.9 | async-start | bytes 8388608 | tf_op jit(solution)/shard_map/while
  321.0 7.0 %slice-start.1 = ((s8[5242880]{0:T(1024)(128)(4,1)}), s8[1048576]{0:T(1024)(128)(4,1)S(1)}, s32[]{:S(2)}) async-start(s8[5242880]{0:T(1024)(128)(4,1)} %bitcast.104), calls=%async_computation.10 | async-start | bytes 2097152 | tf_op jit(solution)/shard_map/while
  340.0 12.0 %slice-start = ((s8[5242880]{0:T(1024)(128)(4,1)}), s8[4194304]{0:T(1024)(128)(4,1)S(1)}, s32[]{:S(2)}) async-start(s8[5242880]{0:T(1024)(128)(4,1)} %bitcast.104), calls=%async_computation.9 | async-start | bytes 8388608 | tf_op jit(solution)/shard_map/while
  343.5 8.5 %slice-start.1 = ((s8[5242880]{0:T(1024)(128)(4,1)}), s8[1048576]{0:T(1024)(128)(4,1)S(1)}, s32[]{:S(2)}) async-start(s8[5242880]{0:T(1024)(128)(4,1)} %bitcast.104), calls=%async_computation.10 | async-start | bytes 2097152 | tf_op jit(solution)/shard_map/while
  364.1 12.0 %slice-start = ((s8[5242880]{0:T(1024)(128)(4,1)}), s8[4194304]{0:T(1024)(128)(4,1)S(1)}, s32[]{:S(2)}) async-start(s8[5242880]{0:T(1024)(128)(4,1)} %bitcast.104), calls=%async_computation.9 | async-start | bytes 8388608 | tf_op jit(solution)/shard_map/while
  367.6 8.5 %slice-start.1 = ((s8[5242880]{0:T(1024)(128)(4,1)}), s8[1048576]{0:T(1024)(128)(4,1)S(1)}, s32[]{:S(2)}) async-start(s8[5242880]{0:T(1024)(128)(4,1)} %bitcast.104), calls=%async_computation.10 | async-start | bytes 2097152 | tf_op jit(solution)/shard_map/while
  388.1 12.0 %slice-start = ((s8[5242880]{0:T(1024)(128)(4,1)}), s8[4194304]{0:T(1024)(128)(4,1)S(1)}, s32[]{:S(2)}) async-start(s8[5242880]{0:T(1024)(128)(4,1)} %bitcast.104), calls=%async_computation.9 | async-start | bytes 8388608 | tf_op jit(solution)/shard_map/while
  391.6 8.5 %slice-start.1 = ((s8[5242880]{0:T(1024)(128)(4,1)}), s8[1048576]{0:T(1024)(128)(4,1)S(1)}, s32[]{:S(2)}) async-start(s8[5242880]{0:T(1024)(128)(4,1)} %bitcast.104), calls=%async_computation.10 | async-start | bytes 2097152 | tf_op jit(solution)/shard_map/while
  413.5 154.5 %all-to-all-start.6 = ((f32[8,16,16,1280]{3,2,0,1:T(8,128)}), f32[8,16,16,1280]{3,2,0,1:T(8,128)}, u32[]{:S(2)}, u32[]{:S(2)}) async-start(f32[8,16,16,1280]{3,2,0,1:T(8,128)} %copy.28), calls=%async_computation.6 | async-start | bytes 20971520 | tf_op jit(solution)/shard_map/all_to_all | solution.py:109
  593.6 16.0 %all-to-all-start.8 = ((bf16[8,2,320]{2,1,0:T(2,128)(2,1)}), bf16[8,2,320]{2,1,0:T(2,128)(2,1)S(1)}, u32[]{:S(2)}, u32[]{:S(2)}) async-start(bf16[8,2,320]{2,1,0:T(2,128)(2,1)} %reshape.179), calls=%async_computation.8 | async-start | bytes 24576 | tf_op jit(solution)/shard_map/all_to_all | solution.py:120
  609.6 24.5 %all-to-all-start.7 = ((bf16[1,8,16,5120]{3,2,0,1:T(8,128)(2,1)}), bf16[1,8,16,5120]{3,2,0,1:T(8,128)(2,1)S(1)}, u32[]{:S(2)}, u32[]{:S(2)}) async-start(bf16[1,8,16,5120]{3,2,0,1:T(8,128)(2,1)} %fusion.10), calls=%async_computation.7 | async-start | bytes 2621440 | tf_op jit(solution)/shard_map/all_to_all | solution.py:119
  619.0 16.2 %copy-start.1 = (s32[8,8]{1,0:T(8,128)S(1)}, s32[8,8]{1,0:T(8,128)}, u32[]{:S(2)}) copy-start(s32[8,8]{1,0:T(8,128)} %param.11) | copy-start | bytes 772
where the time goes:
time: 637 us; the launch traced here: 635 us
  waiting for transfers between devices  342 us (54%)
  local copies, waits for them, and re-layouts  110 us (17%)
  other arithmetic  51.9 us (8%)
  matrix products  50.4 us (8%)
  blocking collectives  47.9 us (8%)
  starting transfers between devices  31.5 us (5%)
    all_to_all x1, waiting for transfers between devices, on_device(): lax.all_to_all(outgoing, 'grid', split_axis=1, concat_axis=1, tiled=True)  132 us
    all_to_all x1, waiting for transfers between devices, on_device(): lax.all_to_all(fan_out(quant_in, row_blocks, GC, True), 'grid', split_axi...  115 us
    all_to_all x1, waiting for transfers between devices, on_device(): lax.all_to_all(fan_out(token_in, row_blocks, GC, False), 'grid', split_ax...  71.9 us
    dot_general x4, matrix products, compute(): jnp.einsum('rkd,rkf->df', inputs, gradient, preferred_element_type=jnp.fl...  32.5 us
    mul x8, local copies, waits for them, and re-layouts, dequantize(): values = values * scales.astype(jnp.float32)[..., None]  29.8 us
    all_to_all x1, blocking collectives, on_device(): lax.all_to_all(tokens, 'grp', split_axis=0, concat_axis=1, tiled=True)  23.5 us
    all_to_all x1, waiting for transfers between devices, on_device(): lax.all_to_all(dy_quant, 'grp', split_axis=0, concat_axis=1, tiled=True)  23.1 us
    dot_general x4, matrix products, compute(): jnp.einsum('rkf,df->rkd', gradient, weight_tile, preferred_element_type=j...  17.9 us
  transfers between devices with their start and end apart: 6, of which 4 were waited for; matrix products, arithmetic and copies ran while one was open for 9% of the time, Pallas kernels for 0%

commit v1 on v0

v1 whole, which is shorter than its diff:
```python
import functools

import jax
import jax.numpy as jnp
from jax import lax
from jax.experimental import pallas as pl
from jax.experimental.pallas import tpu as pltpu
from jax.sharding import PartitionSpec as P

QB = 128
EPS = 1e-06
SIDE = 4
ORDER = (0, 1, 3, 2)
MESH = pl.DeviceIdType.MESH
F32 = jnp.float32
BF16 = jnp.bfloat16


def kernel(
    sizes,
    counts,
    scale,
    dy,
    tokens,
    weight,
    back,
    dw_out,
    dw_scale,
    dy_in,
    grad,
    w_in,
    w_t,
    g_all,
    t_all,
    rs_send,
    rs_recv,
    own_sum,
    back_send,
    dw_sum,
    dw_quant,
    load_sem,
    g_send,
    g_recv,
    t_send,
    t_recv,
    z_send,
    z_recv,
    y_send,
    y_recv,
    r_send,
    r_recv,
    b_send,
    b_recv,
    out_sem,
):
    n_grp, shard, height, breadth = sizes
    nx = n_grp // 2
    chunk = n_grp * shard
    block = SIDE * chunk
    g = lax.axis_index("grp")
    t = lax.axis_index("grid")
    x = g // 2
    c = g % 2
    z = t // SIDE
    y = t % SIDE

    def grp_at(dx, dc):
        return ((x + dx) % nx) * 2 + (c + dc) % 2

    def z_at(d):
        return (z + d) % SIDE

    def y_at(d):
        return (y + d) % SIDE

    x_order = []
    for near in range(1, nx // 2 + 1):
        for dc in range(2):
            x_order.append((near, dc))
            if nx - near != near:
                x_order.append((nx - near, dc))
    x_order += [(0, 1), (0, 0)]

    load_dy = pltpu.make_async_copy(dy, dy_in, load_sem.at[0])
    load_w = pltpu.make_async_copy(weight, w_in, load_sem.at[1])
    load_dy.start()
    load_w.start()

    barrier = pltpu.get_barrier_semaphore()
    partners = 0
    for dx, dc in x_order:
        for d in range(SIDE):
            if (dx, dc, d) != (0, 0, 0):
                pl.semaphore_signal(
                    barrier, inc=1, device_id=(grp_at(dx, dc), z * SIDE + y_at(d)), device_id_type=MESH
                )
                partners += 1
            if d != 0:
                pl.semaphore_signal(
                    barrier, inc=1, device_id=(grp_at(dx, dc), z_at(d) * SIDE + y), device_id_type=MESH
                )
                partners += 1

    load_dy.wait()
    groups = dy_in.shape[1] // QB

    def dequantize(e, carry):
        rows = pl.ds(pl.multiple_of(e * shard, shard), shard)
        live = t * shard + lax.broadcasted_iota(jnp.int32, (shard, groups), 0) < counts[g, e]
        s = jnp.where(live, scale[rows, :].astype(F32), 0.0)
        for j in range(groups):
            cols = slice(j * QB, (j + 1) * QB)
            grad[rows, cols] = (dy_in[rows, cols].astype(F32) * s[:, j : j + 1]).astype(BF16)
        return carry

    lax.fori_loop(0, n_grp, dequantize, 0)
    pl.semaphore_wait(barrier, partners)

    mine = pl.ds(pl.multiple_of(t * chunk + g * shard, shard), shard)
    waits = []

    def remote(src, dst, send, recv, device):
        copy = pltpu.make_async_remote_copy(
            src_ref=src, dst_ref=dst, send_sem=send, recv_sem=recv, device_id=device, device_id_type=MESH
        )
        copy.start()
        waits.append(copy)

    def send_grad(d, index):
        b = y_at(d)
        cols = pl.ds(pl.multiple_of(b * breadth, breadth), breadth)
        for i, (dx, dc) in enumerate(x_order):
            e = grp_at(dx, dc)
            src = grad.at[pl.ds(pl.multiple_of(e * shard, shard), shard), cols]
            if (dx, dc, d) == (0, 0, 0):
                pltpu.make_async_copy(src, g_all.at[mine, :], g_recv.at[y]).start()
            else:
                remote(
                    src, g_all.at[mine, :], g_send.at[index * n_grp + i], g_recv.at[y], (e, z * SIDE + b)
                )

    def send_tokens(d, index):
        a = z_at(d)
        cols = pl.ds(pl.multiple_of(a * height, height), height)
        for i, (dx, dc) in enumerate(x_order):
            e = grp_at(dx, dc)
            src = tokens.at[pl.ds(pl.multiple_of(e * shard, shard), shard), cols]
            if (dx, dc, d) == (0, 0, 0):
                pltpu.make_async_copy(src, t_all.at[mine, :], t_recv.at[z]).start()
            else:
                remote(
                    src, t_all.at[mine, :], t_send.at[index * n_grp + i], t_recv.at[z], (e, a * SIDE + y)
                )

    send_grad(0, 0)
    send_grad(1, 1)
    send_tokens(0, 0)
    send_grad(3, 2)
    send_tokens(1, 1)
    send_grad(2, 3)
    send_tokens(3, 2)
    send_tokens(2, 3)

    load_w.wait()
    step = 256

    def turn(i, carry):
        rows = pl.ds(pl.multiple_of(i * step, step), step)
        for j in range(height // step):
            w_t[rows, j * step : (j + 1) * step] = w_in[j * step : (j + 1) * step, rows].T
        return carry

    lax.fori_loop(0, breadth // step, turn, 0)

    def rows_of(zs, ys):
        return pl.ds(pl.multiple_of((zs * SIDE + ys) * chunk, chunk), chunk)

    def landed(ref, sem):
        pltpu.make_async_copy(ref, ref, sem).wait()

    def input_gradient(kz, k):
        rows = rows_of(z_at(ORDER[kz]), y_at(ORDER[k]))
        slot = kz * 3 + k - 1

        def part(n, carry):
            cols = pl.ds(pl.multiple_of(n * step, step), step)
            p = jnp.dot(g_all[rows, :], w_t[:, cols], preferred_element_type=F32)
            if k == 0:
                own_sum[kz, :, cols] = p
            else:
                rs_send[slot, :, cols] = p.astype(BF16)
            return carry

        lax.fori_loop(0, height // step, part, 0)
        if k != 0:
            remote(
                rs_send.at[slot],
                rs_recv.at[slot],
                r_send.at[slot],
                r_recv.at[slot],
                (g, z * SIDE + y_at(ORDER[k])),
            )

    def reduce(kz):
        for k in range(1, SIDE):
            slot = kz * 3 + k - 1
            landed(rs_recv.at[slot], r_recv.at[slot])
        half = 16

        def part(i, carry):
            rows = pl.ds(pl.multiple_of(i * half, half), half)
            lanes = lax.broadcasted_iota(jnp.int32, (half, QB), 1)
            scales = jnp.zeros((half, QB), F32)
            for j in range(height // QB):
                cols = slice(j * QB, (j + 1) * QB)
                total = own_sum[kz, rows, cols]
                for k in range(1, SIDE):
                    total = total + rs_recv[kz * 3 + k - 1, rows, cols].astype(F32)
                s = jnp.max(jnp.abs(total), axis=1, keepdims=True) + EPS
                back_send[kz, rows, cols] = (total * (1.0 / s)).astype(BF16)
                scales = jnp.where(lanes == j, s, scales)
            back_send[kz, rows, height:] = scales.astype(BF16)
            return carry

        lax.fori_loop(0, chunk // half, part, 0)
        zs = z_at(ORDER[kz])
        dst = back.at[pl.ds(pl.multiple_of((g * SIDE + z) * shard, shard), shard), :]
        for i, (dx, dc) in enumerate(x_order):
            r = grp_at(dx, dc)
            src = back_send.at[kz, pl.ds(pl.multiple_of(r * shard, shard), shard), :]
            if (dx, dc, kz) == (0, 0, 0):
                pltpu.make_async_copy(src, dst, b_recv).start()
            else:
                remote(src, dst, b_send.at[kz * n_grp + i], b_recv, (r, zs * SIDE + y))

    wide = 512

    def weight_gradient(kz, first, last):
        rows = pl.ds(pl.multiple_of(z_at(ORDER[kz]) * block, block), block)

        def row_step(i, carry):
            down = pl.ds(pl.multiple_of(i * step, step), step)

            def col_step(j, carry):
                along = pl.ds(pl.multiple_of(j * wide, wide), wide)
                p = lax.dot_general(
                    t_all[rows, down],
                    g_all[rows, along],
                    (((0,), (0,)), ((), ())),
                    preferred_element_type=F32,
                )
                if not first:
                    p = p + dw_sum[down, along]
                if not last:
                    dw_sum[down, along] = p
                    return carry
                at_row = lax.broadcasted_iota(jnp.int32, dw_scale.shape, 0)
                at_col = lax.broadcasted_iota(jnp.int32, dw_scale.shape, 1)
                scales = dw_scale[...]
                parts = []
                for u in range(step // QB):
                    line = []
                    for v in range(wide // QB):
                        q = p[u * QB : (u + 1) * QB, v * QB : (v + 1) * QB]
                        s = jnp.max(jnp.max(jnp.abs(q), axis=0, keepdims=True), axis=1, keepdims=True) + EPS
                        line.append((q * (1.0 / s)).astype(BF16))
                        here = (at_row == i * (step // QB) + u) & (at_col == j * (wide // QB) + v)
                        scales = jnp.where(here, s, scales)
                    parts.append(jnp.concatenate(line, axis=1))
                dw_scale[...] = scales
                dw_quant[down, along] = jnp.concatenate(parts, axis=0)
                return carry

            lax.fori_loop(0, breadth // wide, col_step, 0)
            if last:
                pltpu.make_async_copy(dw_quant.at[down, :], dw_out.at[down, :], out_sem.at[i]).start()
            return carry

        lax.fori_loop(0, height // step, row_step, 0)

    def pass_grad(rows, up, sem):
        remote(
            g_all.at[rows, :],
            g_all.at[rows, :],
            z_send.at[sem],
            z_recv.at[sem],
            (g, z_at(1 if up else 3) * SIDE + y),
        )

    def pass_tokens(rows, up, sem):
        remote(
            t_all.at[rows, :],
            t_all.at[rows, :],
            y_send.at[sem],
            y_recv.at[sem],
            (g, z * SIDE + y_at(1 if up else 3)),
        )

    for k in range(SIDE):
        rows = rows_of(z, y_at(ORDER[k]))
        landed(g_all.at[rows, :], g_recv.at[y_at(ORDER[k])])
        pass_grad(rows, True, k)
        pass_grad(rows, False, 4 + k)
        rows = rows_of(z_at(ORDER[k]), y)
        landed(t_all.at[rows, :], t_recv.at[z_at(ORDER[k])])
        pass_tokens(rows, True, k)
        pass_tokens(rows, False, 4 + k)
        input_gradient(0, k)

    for k in range(SIDE):
        for up in (True, False):
            rows = rows_of(z_at(3 if up else 1), y_at(ORDER[k]))
            landed(g_all.at[rows, :], z_recv.at[k if up else 4 + k])
            if up == (k % 2 == 0):
                pass_grad(rows, up, 8 + k)
            rows = rows_of(z_at(ORDER[k]), y_at(3 if up else 1))
            landed(t_all.at[rows, :], y_recv.at[k if up else 4 + k])
            if up == (k % 2 == 0):
                pass_tokens(rows, up, 8 + k)
        input_gradient(2, k)
        input_gradient(1, k)

    reduce(0)

    for k in range(SIDE):
        landed(g_all.at[rows_of(z_at(2), y_at(ORDER[k])), :], z_recv.at[8 + k])
        input_gradient(3, k)

    reduce(1)
    reduce(2)
    for k in range(SIDE):
        landed(t_all.at[rows_of(z_at(ORDER[k]), y_at(2)), :], y_recv.at[8 + k])
    weight_gradient(0, True, False)
    weight_gradient(1, False, False)
    reduce(3)
    weight_gradient(2, False, False)
    dw_scale[...] = jnp.zeros(dw_scale.shape, F32)
    weight_gradient(3, False, True)

    for i in range(height // step):
        down = pl.ds(i * step, step)
        pltpu.make_async_copy(dw_quant.at[down, :], dw_out.at[down, :], out_sem.at[i]).wait()
    for copy in waits:
        copy.wait_send()
    landed(back, b_recv)


def on_device(dy_quant, dy_scale, tokens, weight, counts):
    n_grp, _, shard, hidden = dy_quant.shape
    width = tokens.shape[-1]
    height, breadth = weight.shape[-2:]
    rows = n_grp * shard
    slots = SIDE * SIDE * rows
    dma = pltpu.SemaphoreType.DMA
    back, dw_quant, dw_scale = pl.pallas_call(
        functools.partial(kernel, (n_grp, shard, height, breadth)),
        out_shape=(
            jax.ShapeDtypeStruct((n_grp * SIDE * shard, height + QB), BF16),
            jax.ShapeDtypeStruct((height, breadth), BF16),
            jax.ShapeDtypeStruct((height // QB, breadth // QB), F32),
        ),
        in_specs=[
            pl.BlockSpec(memory_space=pltpu.SMEM),
            pl.BlockSpec(memory_space=pltpu.VMEM),
            pl.BlockSpec(memory_space=pl.ANY),
            pl.BlockSpec(memory_space=pl.ANY),
            pl.BlockSpec(memory_space=pl.ANY),
        ],
        out_specs=(
            pl.BlockSpec(memory_space=pl.ANY),
            pl.BlockSpec(memory_space=pl.ANY),
            pl.BlockSpec(memory_space=pltpu.VMEM),
        ),
        scratch_shapes=[
            pltpu.VMEM((rows, hidden), BF16),
            pltpu.VMEM((rows, hidden), BF16),
            pltpu.VMEM((height, breadth), BF16),
            pltpu.VMEM((breadth, height), BF16),
            pltpu.VMEM((slots, breadth), BF16),
            pltpu.VMEM((slots, height), BF16),
            pltpu.VMEM((12, rows, height), BF16),
            pltpu.VMEM((12, rows, height), BF16),
            pltpu.VMEM((SIDE, rows, height), F32),
            pltpu.VMEM((SIDE, rows, height + QB), BF16),
            pltpu.VMEM((height, breadth), F32),
            pltpu.VMEM((height, breadth), BF16),
            dma((2,)),
            dma((SIDE * n_grp,)),
            dma((SIDE,)),
            dma((SIDE * n_grp,)),
            dma((SIDE,)),
            dma((12,)),
            dma((12,)),
            dma((12,)),
            dma((12,)),
            dma((12,)),
            dma((12,)),
            dma((SIDE * n_grp,)),
            dma,
            dma((height // 256,)),
        ],
        compiler_params=pltpu.CompilerParams(
            collective_id=0, has_side_effects=True, vmem_limit_bytes=62 * 2**20
        ),
        name="up_backward",
    )(
        counts,
        dy_scale.reshape(rows, hidden // QB),
        dy_quant.reshape(rows, hidden),
        tokens.reshape(rows, width),
        weight.reshape(height, breadth),
    )
    parts = back.reshape(n_grp, SIDE, shard, height + QB)
    dx_quant = jnp.swapaxes(parts[..., :height], 1, 2).reshape(n_grp, 1, shard, width)
    dx_scale = jnp.swapaxes(parts[..., height : height + height // QB], 1, 2)
    return (
        dx_quant,
        dx_scale.reshape(n_grp, 1, shard, width // QB),
        dw_quant[None, None],
        dw_scale[None, None],
    )


def solution(mesh):
    return jax.shard_map(
        on_device,
        mesh=mesh,
        in_specs=(
            P(None, "grp", "grid", None),
            P(None, "grp", "grid", None),
            P(None, "grp", "grid", None),
            P("grp", "grid", None, None),
            P(),
        ),
        out_specs=(
            P(None, "grp", "grid", None),
            P(None, "grp", "grid", None),
            P("grp", "grid", None, None),
            P("grp", "grid", None, None),
        ),
        check_vma=False,
    )
```

time: 637 us -> 179 us (0.28)
  waiting for transfers between devices: 342 us -> 0 us
  Pallas kernels: 0 us -> 165 us
  local copies, waits for them, and re-layouts: 110 us -> 12.2 us
  other arithmetic: 51.9 us -> 0 us
  matrix products: 50.4 us -> 0 us
  blocking collectives: 47.9 us -> 0 us
  starting transfers between devices: 31.5 us -> 0 us
    all_to_all x6 -> x0, waiting for transfers between devices: 342 us -> none  [the longest x1 132 us: on_device(): lax.all_to_all(outgoing, 'grid', split_axis=1, concat_axis=1, tiled=True)]
    pallas_call x0 -> x1, Pallas kernels: none -> 165 us  [on_device(): pl.pallas_call(functools.partial(kernel, (n_grp, shard, height, breadth))...]
    dot_general x8 -> x0, matrix products: 50.4 us -> none  [the longest x4 32.5 us: compute(): jnp.einsum('rkd,rkf->df', inputs, gradient, preferred_element_type=jnp.fl...]
    all_to_all x3 -> x0, blocking collectives: 47.9 us -> none  [the longest x1 23.5 us: on_device(): lax.all_to_all(tokens, 'grp', split_axis=0, concat_axis=1, tiled=True)]
    all_to_all x6 -> x0, starting transfers between devices: 31.5 us -> none  [the longest x1 7.32 us: on_device(): lax.all_to_all(scale_x.astype(jnp.bfloat16)[None], 'grp', split_axis=1, c...]
    mul x8 -> x0, local copies, waits for them, and re-layouts: 29.8 us -> none  [dequantize(): values = values * scales.astype(jnp.float32)[..., None]]
    convert_element_type x10 -> x0, other arithmetic: 17.4 us -> none  [the longest x4 14 us: dequantize(): jnp.where(live[:, :, None], values.reshape(replicas, rows, hidden), 0.0)]
    broadcast_in_dim x7 -> x0, local copies, waits for them, and re-layouts: 16.4 us -> none  [the longest x4 7.25 us: fan_out(): jnp.broadcast_to(split[..., None, :, :, :], lead + (row_blocks, col_block...]
  transfers between devices with their start and end apart: 6 -> 0, of which waited for: 4 -> 0; matrix products, arithmetic and copies ran while one was open for 9% -> 0% of each run, Pallas kernels for 0% -> 0%
where the time goes in v1:
time: 179 us; the launch traced here: 178 us
  Pallas kernels  165 us (92%)
  local copies, waits for them, and re-layouts  12.2 us (7%)
    pallas_call x1, Pallas kernels, on_device(): pl.pallas_call(functools.partial(kernel, (n_grp, shard, height, breadth))...  165 us
    unnamed x6, local copies, waits for them, and re-layouts  7.31 us

profile of v1, /device:TPU:1, one launch (start us, length us, event | category | flops | bytes accessed | tf_op | source)
XLA Modules:
  0.0 178.2 jit_solution(6184019943100282639)
XLA Ops:
  0.6 165.3 %up_backward.1 = (bf16[512,1408]{1,0:T(8,128)(2,1)}, bf16[1280,2048]{1,0:T(8,128)(2,1)}, f32[10,16]{1,0:T(8,128)}) custom-call(s32[8,8]{1,0:T(8,128)} %counts.1, bf16[128,64]{1,0:T(8,128)(2,1)} %bitcast.19, bf16[128,8192]{1,0:T(8,128)(2,1)} %bitcast.14, bf16[128,5120]{1,0:T(8,128)(2,1)} %bitcast.17, bf16[1280,2048]{1,0:T(8,128)(2,1)} %bitcast.13), custom_call_target="tpu_custom_call" | custom-call | tf_op jit(solution)/shard_map/up_backward/pallas_call | solution.py:355
  166.0 1.4 slice_bitcast_fusion
  167.4 0.7 copy.12
  168.1 0.0 copy-start
  168.1 1.8 %reshape.34 = bf16[8,1,16,5120]{3,2,1,0:T(8,128)(2,1)} reshape(bf16[8,16,4,1280]{3,2,1,0:T(4,128)(2,1)S(1)} %copy.12) | data formatting | bytes 2621440 | tf_op jit(solution)/shard_map/reshape | solution.py:414
  170.0 0.9 slice.9
  170.9 0.3 copy.16
  171.2 0.7 copy.14
  171.9 0.0 copy-done
  171.9 0.6 copy.15
  172.5 5.7 %copy.18 = bf16[1,1,1280,2048]{3,2,1,0:T(8,128)(2,1)} copy(bf16[1,1,1280,2048]{3,2,1,0:T(8,128)(2,1)} %bitcast.12) | data formatting | bytes 10485760
Async XLA Ops:
  168.1 3.8 %copy-start = (f32[10,16]{1,0:T(8,128)S(1)}, f32[10,16]{1,0:T(8,128)}, u32[]{:S(2)}) copy-start(f32[10,16]{1,0:T(8,128)} %get-tuple-element.9) | copy-start | bytes 1924

commit v2 on v1

v2 whole, which is shorter than its diff:
```python
import functools

import jax
import jax.numpy as jnp
from jax import lax
from jax.experimental import pallas as pl
from jax.experimental.pallas import tpu as pltpu
from jax.sharding import PartitionSpec as P

QB = 128
EPS = 1e-06
SIDE = 4
ORDER = (0, 1, 3, 2)

STEPS = (
    ("grad", 3),
    ("tokens", 1),
    ("tokens", 2),
    ("tokens", 3),
    ("tokens", 0),
    ("grad", 1),
    ("grad", 2),
    ("grad", 0),
    ("turn", ),
    ("grad_own", 3),
    ("dx", 0, 3),
    ("tokens_own", 1),
    ("tokens_own", 2),
    ("tokens_own", 3),
    ("tokens_own", 0),
    ("grad_own", 1),
    ("dx", 0, 1),
    ("tokens_near", 1),
    ("grad_own", 2),
    ("dx", 0, 2),
    ("tokens_near", 2),
    ("grad_own", 0),
    ("dx", 0, 0),
    ("tokens_near", 3),
    ("reduce", 0),
    ("grad_near", 3),
    ("grad_on", 3),
    ("dx", 1, 3),
    ("dx", 2, 3),
    ("tokens_near", 0),
    ("grad_near", 1),
    ("grad_on", 1),
    ("dx", 1, 1),
    ("dx", 2, 1),
    ("grad_near", 2),
    ("grad_on", 2),
    ("dx", 1, 2),
    ("dx", 2, 2),
    ("grad_near", 0),
    ("grad_on", 0),
    ("dx", 1, 0),
    ("dx", 2, 0),
    ("grad_far", 3),
    ("dx", 3, 3),
    ("tokens_far", 1),
    ("tokens_far", 2),
    ("tokens_far", 3),
    ("tokens_far", 0),
    ("turn_tokens", 0),
    ("turn_tokens", 1),
    ("turn_tokens", 2),
    ("turn_tokens", 3),
    ("dw", 0, True, False),
    ("reduce", 1),
    ("reduce", 2),
    ("grad_far", 1),
    ("dx", 3, 1),
    ("grad_far", 2),
    ("dx", 3, 2),
    ("grad_far", 0),
    ("dx", 3, 0),
    ("dw", 1, False, False),
    ("reduce", 3),
    ("dw", 2, False, False),
    ("dw", 3, False, True),
)
MESH = pl.DeviceIdType.MESH
F32 = jnp.float32
BF16 = jnp.bfloat16


def kernel(
    sizes,
    counts,
    scale,
    dy,
    tokens,
    weight,
    back,
    dw_out,
    dw_scale,
    dy_in,
    grad,
    w_in,
    w_t,
    g_all,
    t_all,
    rs_send,
    rs_half,
    rs_recv,
    own_sum,
    back_send,
    dw_sum,
    dw_quant,
    load_sem,
    g_send,
    g_recv,
    t_send,
    t_recv,
    z_send,
    z_recv,
    y_send,
    y_recv,
    h_send,
    h_recv,
    r_send,
    r_recv,
    b_send,
    b_recv,
    out_sem,
):
    n_grp, shard, height, breadth = sizes
    nx = n_grp // 2
    chunk = n_grp * shard
    block = SIDE * chunk
    g = lax.axis_index("grp")
    t = lax.axis_index("grid")
    x = g // 2
    c = g % 2
    z = t // SIDE
    y = t % SIDE

    def grp_at(dx, dc):
        return ((x + dx) % nx) * 2 + (c + dc) % 2

    def z_at(d):
        return (z + d + SIDE) % SIDE

    def y_at(d):
        return (y + d + SIDE) % SIDE

    x_order = []
    for near in range(1, nx // 2 + 1):
        for dc in range(2):
            x_order.append((near, dc))
            if nx - near != near:
                x_order.append((nx - near, dc))
    x_order += [(0, 1), (0, 0)]

    load_dy = pltpu.make_async_copy(dy, dy_in, load_sem.at[0])
    load_w = pltpu.make_async_copy(weight, w_in, load_sem.at[1])
    load_dy.start()
    load_w.start()

    barrier = pltpu.get_barrier_semaphore()
    partners = 0
    for dx, dc in x_order:
        for d in range(SIDE):
            if (dx, dc, d) != (0, 0, 0):
                pl.semaphore_signal(
                    barrier, inc=1, device_id=(grp_at(dx, dc), z * SIDE + y_at(d)), device_id_type=MESH
                )
                partners += 1
            if d != 0:
                pl.semaphore_signal(
                    barrier, inc=1, device_id=(grp_at(dx, dc), z_at(d) * SIDE + y), device_id_type=MESH
                )
                partners += 1

    load_dy.wait()
    groups = dy_in.shape[1] // QB

    def dequantize(e, carry):
        rows = pl.ds(pl.multiple_of(e * shard, shard), shard)
        live = t * shard + lax.broadcasted_iota(jnp.int32, (shard, groups), 0) < counts[g, e]
        s = jnp.where(live, scale[rows, :].astype(F32), 0.0)
        for j in range(groups):
            cols = slice(j * QB, (j + 1) * QB)
            grad[rows, cols] = (dy_in[rows, cols].astype(F32) * s[:, j : j + 1]).astype(BF16)
        return carry

    lax.fori_loop(0, n_grp, dequantize, 0)
    pl.semaphore_wait(barrier, partners)

    mine = pl.ds(pl.multiple_of(t * chunk + g * shard, shard), shard)
    waits = []

    def remote(src, dst, send, recv, device, to=None):
        copy = pltpu.make_async_remote_copy(
            src_ref=src, dst_ref=dst, send_sem=send, recv_sem=recv, device_id=device, device_id_type=MESH
        )
        copy.start()
        (waits if to is None else to).append(copy)

    in_flight = {}

    def send_grad(index):
        d = ORDER[index]
        b = y_at(d)
        sent = in_flight["grad", index] = []
        cols = pl.ds(pl.multiple_of(b * breadth, breadth), breadth)
        for i, (dx, dc) in enumerate(x_order):
            e = grp_at(dx, dc)
            src = grad.at[pl.ds(pl.multiple_of(e * shard, shard), shard), cols]
            if (dx, dc, d) == (0, 0, 0):
                pltpu.make_async_copy(src, g_all.at[mine, :], g_recv.at[y]).start()
            else:
                remote(
                    src, g_all.at[mine, :], g_send.at[index * n_grp + i], g_recv.at[y], (e, z * SIDE + b), sent
                )

    def send_tokens(index):
        d = ORDER[index]
        a = z_at(d)
        sent = in_flight["tokens", index] = []
        cols = pl.ds(pl.multiple_of(a * height, height), height)
        for i, (dx, dc) in enumerate(x_order):
            e = grp_at(dx, dc)
            src = tokens.at[pl.ds(pl.multiple_of(e * shard, shard), shard), cols]
            if (dx, dc, d) == (0, 0, 0):
                pltpu.make_async_copy(src, t_all.at[mine, :], t_recv.at[z]).start()
            else:
                remote(
                    src, t_all.at[mine, :], t_send.at[index * n_grp + i], t_recv.at[z], (e, a * SIDE + y), sent
                )

    def sent(name, index):
        for copy in in_flight.pop((name, index)):
            copy.wait_send()

    step = 256

    def turn(i, carry):
        rows = pl.ds(pl.multiple_of(i * step, step), step)
        for j in range(height // step):
            w_t[rows, j * step : (j + 1) * step] = w_in[j * step : (j + 1) * step, rows].T
        return carry

    def turn_weight():
        load_w.wait()
        lax.fori_loop(0, breadth // step, turn, 0)

    def rows_of(zs, ys):
        return pl.ds(pl.multiple_of((zs * SIDE + ys) * chunk, chunk), chunk)

    def landed(ref, sem):
        pltpu.make_async_copy(ref, ref, sem).wait()

    def cut_of(kz):
        return (3 if kz in (0, 3) else 2) * step

    def cut_of(kz):
        return (3 if kz in (0, 3) else 2) * step

    def input_gradient(kz, k):
        cut = cut_of(kz)
        halves = {1: slice(cut, height), 2: slice(0, cut)}
        p = jnp.dot(g_all[rows_of(z_at(ORDER[kz]), y_at(ORDER[k])), :], w_t[...], preferred_element_type=F32)
        if k == 0:
            own_sum[kz] = p
            return
        slot = kz * 3 + k - 1
        src = rs_send.at[slot]
        if k == 3:
            rs_send[slot] = p.astype(BF16)
            for way, d in ((0, 3), (1, 1)):
                cols = halves[2 - way]
                sem = kz * 2 + way
                remote(
                    src.at[:, cols],
                    rs_half.at[kz, :, cols],
                    h_send.at[sem],
                    h_recv.at[sem],
                    (g, z * SIDE + y_at(d)),
                )
            return
        other = halves[3 - k]
        cols = halves[k]
        rs_send[slot, :, other] = p[:, other].astype(BF16)
        landed(rs_half.at[kz, :, cols], h_recv.at[kz * 2 + k % 2])
        rs_send[slot, :, cols] = (p[:, cols] + rs_half[kz, :, cols].astype(F32)).astype(BF16)
        slot = kz * 2 + k - 1
        remote(src, rs_recv.at[slot], r_send.at[slot], r_recv.at[slot], (g, z * SIDE + y_at(ORDER[k])))

    def reduce(kz):
        for slot in (kz * 2, kz * 2 + 1):
            landed(rs_recv.at[slot], r_recv.at[slot])
        half = 16

        def part(i, carry):
            rows = pl.ds(pl.multiple_of(i * half, half), half)
            lanes = lax.broadcasted_iota(jnp.int32, (half, QB), 1)
            scales = jnp.zeros((half, QB), F32)
            for j in range(height // QB):
                cols = slice(j * QB, (j + 1) * QB)
                total = own_sum[kz, rows, cols]
                for slot in (kz * 2, kz * 2 + 1):
                    total = total + rs_recv[slot, rows, cols].astype(F32)
                s = jnp.max(jnp.abs(total), axis=1, keepdims=True) + EPS
                back_send[kz, rows, cols] = (total * (1.0 / s)).astype(BF16)
                scales = jnp.where(lanes == j, s, scales)
            back_send[kz, rows, height:] = scales.astype(BF16)
            return carry

        lax.fori_loop(0, chunk // half, part, 0)
        zs = z_at(ORDER[kz])
        dst = back.at[pl.ds(pl.multiple_of((g * SIDE + z) * shard, shard), shard), :]
        for i, (dx, dc) in enumerate(x_order):
            r = grp_at(dx, dc)
            src = back_send.at[kz, pl.ds(pl.multiple_of(r * shard, shard), shard), :]
            if (dx, dc, kz) == (0, 0, 0):
                pltpu.make_async_copy(src, dst, b_recv).start()
            else:
                remote(src, dst, b_send.at[kz * n_grp + i], b_recv, (r, zs * SIDE + y))

    wide = 512

    def turn_tokens(kz):
        for u in range(block // step):
            rows = pl.ds(pl.multiple_of(z_at(ORDER[kz]) * block + u * step, step), step)

            def turn(i, carry):
                down = pl.ds(pl.multiple_of(i * step, step), step)
                w_in[down, rows] = t_all[rows, down].T
                return carry

            lax.fori_loop(0, height // step, turn, 0)

    def weight_gradient(kz, first, last):
        rows = pl.ds(pl.multiple_of(z_at(ORDER[kz]) * block, block), block)

        def col_step(j, carry):
            along = pl.ds(pl.multiple_of(j * wide, wide), wide)
            p = jnp.dot(w_in[:, rows], g_all[rows, along], preferred_element_type=F32)
            if not first:
                p = p + dw_sum[:, along]
            if not last:
                dw_sum[:, along] = p
                return carry
            at_row = lax.broadcasted_iota(jnp.int32, dw_scale.shape, 0)
            at_col = lax.broadcasted_iota(jnp.int32, dw_scale.shape, 1)
            scales = dw_scale[...]
            for u in range(height // QB):
                for v in range(wide // QB):
                    q = p[u * QB : (u + 1) * QB, v * QB : (v + 1) * QB]
                    s = jnp.max(jnp.max(jnp.abs(q), axis=0, keepdims=True), axis=1, keepdims=True) + EPS
                    cols = pl.ds(pl.multiple_of(j * wide + v * QB, QB), QB)
                    dw_quant[u * QB : (u + 1) * QB, cols] = (q * (1.0 / s)).astype(BF16)
                    scales = jnp.where((at_row == u) & (at_col == j * (wide // QB) + v), s, scales)
            dw_scale[...] = scales
            pltpu.make_async_copy(dw_quant.at[:, along], dw_out.at[:, along], out_sem.at[j]).start()
            return carry

        lax.fori_loop(0, breadth // wide, col_step, 0)

    def half_of(zs, ys, upper):
        start = (zs * SIDE + ys) * chunk + (chunk // 2 if upper else 0)
        return pl.ds(pl.multiple_of(start, chunk // 2), chunk // 2)

    def pass_on(buffer, rows, send, recv, device):
        remote(buffer.at[rows, :], buffer.at[rows, :], send, recv, device)

    def grad_own(k):
        rows = rows_of(z, y_at(ORDER[k]))
        landed(g_all.at[rows, :], g_recv.at[y_at(ORDER[k])])
        for way, d in enumerate((1, 3)):
            sem = way * SIDE + k
            pass_on(g_all, rows, z_send.at[sem], z_recv.at[sem], (g, z_at(d) * SIDE + y))

    def grad_near(k):
        for way, d in enumerate((1, 3)):
            landed(g_all.at[rows_of(z_at(-d), y_at(ORDER[k])), :], z_recv.at[way * SIDE + k])

    def grad_on(k):
        for way, d in enumerate((1, 3)):
            rows = half_of(z_at(-d), y_at(ORDER[k]), way == 0)
            sem = (2 + way) * SIDE + k
            pass_on(g_all, rows, z_send.at[sem], z_recv.at[sem], (g, z_at(d) * SIDE + y))

    def grad_far(k):
        for way in range(2):
            rows = half_of(z_at(2), y_at(ORDER[k]), way == 0)
            landed(g_all.at[rows, :], z_recv.at[(2 + way) * SIDE + k])

    def tokens_own(k):
        rows = rows_of(z_at(ORDER[k]), y)
        landed(t_all.at[rows, :], t_recv.at[z_at(ORDER[k])])
        for way, d in enumerate((1, 3)):
            sem = way * SIDE + k
            pass_on(t_all, rows, y_send.at[sem], y_recv.at[sem], (g, z * SIDE + y_at(d)))

    def tokens_near(k):
        for way, d in enumerate((1, 3)):
            landed(t_all.at[rows_of(z_at(ORDER[k]), y_at(-d)), :], y_recv.at[way * SIDE + k])
            rows = half_of(z_at(ORDER[k]), y_at(-d), way == 0)
            sem = (2 + way) * SIDE + k
            pass_on(t_all, rows, y_send.at[sem], y_recv.at[sem], (g, z * SIDE + y_at(d)))

    def tokens_far(k):
        for way in range(2):
            rows = half_of(z_at(ORDER[k]), y_at(2), way == 0)
            landed(t_all.at[rows, :], y_recv.at[(2 + way) * SIDE + k])

    dw_scale[...] = jnp.zeros(dw_scale.shape, F32)
    actions = {
        "grad": send_grad,
        "tokens": send_tokens,
        "grad_sent": functools.partial(sent, "grad"),
        "tokens_sent": functools.partial(sent, "tokens"),
        "turn": turn_weight,
        "grad_own": grad_own,
        "grad_near": grad_near,
        "grad_on": grad_on,
        "turn_tokens": turn_tokens,
        "grad_far": grad_far,
        "tokens_own": tokens_own,
        "tokens_near": tokens_near,
        "tokens_far": tokens_far,
        "dx": input_gradient,
        "reduce": reduce,
        "dw": weight_gradient,
    }
    for name, *numbers in STEPS:
        actions[name](*numbers)

    for j in range(breadth // wide):
        along = pl.ds(j * wide, wide)
        pltpu.make_async_copy(dw_quant.at[:, along], dw_out.at[:, along], out_sem.at[j]).wait()
    for copy in sum(in_flight.values(), waits):
        copy.wait_send()
    landed(back, b_recv)


def on_device(dy_quant, dy_scale, tokens, weight, counts):
    n_grp, _, shard, hidden = dy_quant.shape
    width = tokens.shape[-1]
    height, breadth = weight.shape[-2:]
    rows = n_grp * shard
    slots = SIDE * SIDE * rows
    dma = pltpu.SemaphoreType.DMA
    back, dw_quant, dw_scale = pl.pallas_call(
        functools.partial(kernel, (n_grp, shard, height, breadth)),
        out_shape=(
            jax.ShapeDtypeStruct((n_grp * SIDE * shard, height + QB), BF16),
            jax.ShapeDtypeStruct((height, breadth), BF16),
            jax.ShapeDtypeStruct((height // QB, breadth // QB), F32),
        ),
        in_specs=[
            pl.BlockSpec(memory_space=pltpu.SMEM),
            pl.BlockSpec(memory_space=pltpu.VMEM),
            pl.BlockSpec(memory_space=pl.ANY),
            pl.BlockSpec(memory_space=pl.ANY),
            pl.BlockSpec(memory_space=pl.ANY),
        ],
        out_specs=(
            pl.BlockSpec(memory_space=pl.ANY),
            pl.BlockSpec(memory_space=pl.ANY),
            pl.BlockSpec(memory_space=pltpu.VMEM),
        ),
        scratch_shapes=[
            pltpu.VMEM((rows, hidden), BF16),
            pltpu.VMEM((rows, hidden), BF16),
            pltpu.VMEM((height, breadth), BF16),
            pltpu.VMEM((breadth, height), BF16),
            pltpu.VMEM((slots, breadth), BF16),
            pltpu.VMEM((slots, height), BF16),
            pltpu.VMEM((12, rows, height), BF16),
            pltpu.VMEM((SIDE, rows, height), BF16),
            pltpu.VMEM((8, rows, height), BF16),
            pltpu.VMEM((SIDE, rows, height), F32),
            pltpu.VMEM((SIDE, rows, height + QB), BF16),
            pltpu.VMEM((height, breadth), F32),
            pltpu.VMEM((height, breadth), BF16),
            dma((2,)),
            dma((SIDE * n_grp,)),
            dma((SIDE,)),
            dma((SIDE * n_grp,)),
            dma((SIDE,)),
            dma((16,)),
            dma((16,)),
            dma((16,)),
            dma((16,)),
            dma((8,)),
            dma((8,)),
            dma((8,)),
            dma((8,)),
            dma((SIDE * n_grp,)),
            dma,
            dma((breadth // 512,)),
        ],
        compiler_params=pltpu.CompilerParams(
            collective_id=0, has_side_effects=True, vmem_limit_bytes=62 * 2**20
        ),
        name="up_backward",
    )(
        counts,
        dy_scale.reshape(rows, hidden // QB),
        dy_quant.reshape(rows, hidden),
        tokens.reshape(rows, width),
        weight.reshape(height, breadth),
    )
    dx_quant, dx_scale, dw_quant = finish(
        back.reshape(n_grp, SIDE, shard, height + QB), dw_quant
    )
    return (dx_quant[:, None], dx_scale[:, None], dw_quant[None, None], dw_scale[None, None])


def finish_kernel(back, dw, dx_out, scale_out, dw_out, scales, dx, dw_in, scale_sem, dx_sem, dw_sem):
    n_grp, parts, shard, width = back.shape
    height = width - QB
    groups = height // QB
    loads = []
    for a in range(parts):
        cols = slice(a * height, (a + 1) * height)
        loads.append(pltpu.make_async_copy(back.at[:, a, :, :height], dx.at[:, :, cols], dx_sem.at[0, a]))
    piece = dw.shape[0] // dw_sem.shape[1]
    for i in range(dw_sem.shape[1]):
        rows = slice(i * piece, (i + 1) * piece)
        loads.append(pltpu.make_async_copy(dw.at[rows], dw_in.at[rows], dw_sem.at[0, i]))
    load = pltpu.make_async_copy(back.at[:, :, :, height:], scales, scale_sem)
    for copy in loads:
        copy.start()
    load.start()
    copies = []
    for a in range(parts):
        loads[a].wait()
    for a in range(2):
        part = slice(a * n_grp // 2, (a + 1) * n_grp // 2)
        copies.append(pltpu.make_async_copy(dx.at[part], dx_out.at[part], dx_sem.at[1, a]))
        copies[-1].start()
    for i in range(dw_sem.shape[1]):
        loads[parts + i].wait()
        rows = slice(i * piece, (i + 1) * piece)
        copies.append(pltpu.make_async_copy(dw_in.at[rows], dw_out.at[rows], dw_sem.at[1, i]))
        copies[-1].start()
    load.wait()
    for e in range(n_grp):
        line = [scales[e, a][:, :groups] for a in range(parts)]
        scale_out[e] = jnp.concatenate(line, axis=1)
    for copy in copies:
        copy.wait()


def finish(back, dw):
    n_grp, parts, shard, width = back.shape
    height = width - QB
    anywhere = pl.BlockSpec(memory_space=pl.ANY)
    dma = pltpu.SemaphoreType.DMA
    return pl.pallas_call(
        finish_kernel,
        out_shape=(
            jax.ShapeDtypeStruct((n_grp, shard, parts * height), BF16),
            jax.ShapeDtypeStruct((n_grp, shard, parts * height // QB), BF16),
            jax.ShapeDtypeStruct(dw.shape, BF16),
        ),
        in_specs=[anywhere, anywhere],
        out_specs=(anywhere, pl.BlockSpec(memory_space=pltpu.VMEM), anywhere),
        scratch_shapes=[
            pltpu.VMEM((n_grp, parts, shard, QB), BF16),
            pltpu.VMEM((n_grp, shard, parts * height), BF16),
            pltpu.VMEM(dw.shape, BF16),
            dma,
            dma((2, parts)),
            dma((2, 5)),
        ],
        compiler_params=pltpu.CompilerParams(vmem_limit_bytes=62 * 2**20),
        name="finish",
    )(back, dw)


def solution(mesh):
    return jax.shard_map(
        on_device,
        mesh=mesh,
        in_specs=(
            P(None, "grp", "grid", None),
            P(None, "grp", "grid", None),
            P(None, "grp", "grid", None),
            P("grp", "grid", None, None),
            P(),
        ),
        out_specs=(
            P(None, "grp", "grid", None),
            P(None, "grp", "grid", None),
            P("grp", "grid", None, None),
            P("grp", "grid", None, None),
        ),
        check_vma=False,
    )
```

time: 179 us -> 145 us (0.81)
  Pallas kernels: 165 us -> 143 us
  local copies, waits for them, and re-layouts: 12.2 us -> 0.6 us
    pallas_call x1, Pallas kernels: 165 us -> 137 us  [on_device(): pl.pallas_call(functools.partial(kernel, (n_grp, shard, height, breadth))...]
    unnamed x6 -> x3, local copies, waits for them, and re-layouts: 7.31 us -> 0.6 us
    pallas_call x0 -> x1, Pallas kernels: none -> 6.31 us  [finish(): pl.pallas_call(finish_kernel, out_shape=(jax.ShapeDtypeStruct((n_grp, sha...]
    transpose x2 -> x0, local copies, waits for them, and re-layouts: 2.11 us -> none  [on_device(): jnp.swapaxes(parts[..., :height], 1, 2).reshape(n_grp, 1, shard, width)]
    reshape x1 -> x0, local copies, waits for them, and re-layouts: 1.84 us -> none  [on_device(): jnp.swapaxes(parts[..., :height], 1, 2).reshape(n_grp, 1, shard, width)]
where the time goes in v2:
time: 145 us
  Pallas kernels  143 us (99%)
    pallas_call x1, Pallas kernels, on_device(): pl.pallas_call(functools.partial(kernel, (n_grp, shard, height, breadth))...  137 us
    pallas_call x1, Pallas kernels, finish(): pl.pallas_call(finish_kernel, out_shape=(jax.ShapeDtypeStruct((n_grp, sha...  6.31 us

profile of v2, /device:TPU:1, one launch (start us, length us, event | category | flops | bytes accessed | tf_op | source)
XLA Modules:
  0.0 144.5 jit_solution(15883091301921403304)
XLA Ops:
  0.6 137.0 %up_backward.1 = (bf16[512,1408]{1,0:T(8,128)(2,1)}, bf16[1280,2048]{1,0:T(8,128)(2,1)}, f32[10,16]{1,0:T(8,128)}) custom-call(s32[8,8]{1,0:T(8,128)} %counts.1, bf16[128,64]{1,0:T(8,128)(2,1)} %bitcast.17, bf16[128,8192]{1,0:T(8,128)(2,1)} %bitcast.14, bf16[128,5120]{1,0:T(8,128)(2,1)} %bitcast.16, bf16[1280,2048]{1,0:T(8,128)(2,1)} %bitcast.13), custom_call_target="tpu_custom_call" | custom-call | tf_op jit(solution)/shard_map/up_backward/pallas_call | solution.py:446
  137.6 0.0 copy-start
  137.6 6.3 %finish.1 = (bf16[8,16,5120]{2,1,0:T(8,128)(2,1)}, bf16[8,16,40]{2,1,0:T(8,128)(2,1)}, bf16[1280,2048]{1,0:T(8,128)(2,1)}) custom-call(bf16[8,4,16,1408]{3,2,1,0:T(8,128)(2,1)} %bitcast.15, bf16[1280,2048]{1,0:T(8,128)(2,1)} %get-tuple-element.11.dw), custom_call_target="tpu_custom_call" | custom-call | tf_op jit(solution)/shard_map/finish/pallas_call | solution.py:554
  143.9 0.0 copy-done
  143.9 0.6 copy.11
Async XLA Ops:
  137.6 6.3 %copy-start = (f32[10,16]{1,0:T(8,128)S(1)}, f32[10,16]{1,0:T(8,128)}, u32[]{:S(2)}) copy-start(f32[10,16]{1,0:T(8,128)} %get-tuple-element.15) | copy-start | bytes 1924

commit v3 on v2

--- a/solution.py
+++ b/solution.py
@@ -16,37 +16,35 @@
     ("grad", 3),
     ("tokens", 1),
     ("tokens", 2),
+    ("grad", 1),
+    ("grad", 2),
     ("tokens", 3),
     ("tokens", 0),
-    ("grad", 1),
-    ("grad", 2),
     ("grad", 0),
     ("turn", ),
     ("grad_own", 3),
     ("dx", 0, 3),
     ("tokens_own", 1),
     ("tokens_own", 2),
+    ("grad_own", 1),
+    ("dx", 0, 1),
+    ("grad_own", 2),
+    ("dx", 0, 2),
+    ("grad_own", 0),
+    ("dx", 0, 0),
     ("tokens_own", 3),
     ("tokens_own", 0),
-    ("grad_own", 1),
-    ("dx", 0, 1),
-    ("tokens_near", 1),
-    ("grad_own", 2),
-    ("dx", 0, 2),
-    ("tokens_near", 2),
-    ("grad_own", 0),
-    ("dx", 0, 0),
-    ("tokens_near", 3),
     ("reduce", 0),
     ("grad_near", 3),
     ("grad_on", 3),
     ("dx", 1, 3),
     ("dx", 2, 3),
-    ("tokens_near", 0),
+    ("tokens_near", 1),
     ("grad_near", 1),
     ("grad_on", 1),
     ("dx", 1, 1),
     ("dx", 2, 1),
+    ("tokens_near", 2),
     ("grad_near", 2),
     ("grad_on", 2),
     ("dx", 1, 2),
@@ -57,27 +55,29 @@
     ("dx", 2, 0),
     ("grad_far", 3),
     ("dx", 3, 3),
-    ("tokens_far", 1),
-    ("tokens_far", 2),
-    ("tokens_far", 3),
-    ("tokens_far", 0),
-    ("turn_tokens", 0),
-    ("turn_tokens", 1),
-    ("turn_tokens", 2),
-    ("turn_tokens", 3),
-    ("dw", 0, True, False),
     ("reduce", 1),
     ("reduce", 2),
     ("grad_far", 1),
     ("dx", 3, 1),
     ("grad_far", 2),
     ("dx", 3, 2),
+    ("tokens_near", 3),
+    ("tokens_near", 0),
+    ("tokens_far", 1),
+    ("turn_tokens", 1),
+    ("dw", 1, True, False),
     ("grad_far", 0),
     ("dx", 3, 0),
-    ("dw", 1, False, False),
+    ("tokens_far", 2),
+    ("turn_tokens", 2),
+    ("dw", 2, False, False),
     ("reduce", 3),
-    ("dw", 2, False, False),
-    ("dw", 3, False, True),
+    ("tokens_far", 3),
+    ("turn_tokens", 3),
+    ("dw", 3, False, False),
+    ("tokens_far", 0),
+    ("turn_tokens", 0),
+    ("dw", 0, False, True),
 )
 MESH = pl.DeviceIdType.MESH
 F32 = jnp.float32

time: 145 us -> 139 us (0.959)
  Pallas kernels: 143 us -> 137 us
    pallas_call x1, Pallas kernels: 137 us -> 131 us  [on_device(): pl.pallas_call(functools.partial(kernel, (n_grp, shard, height, breadth))...]
where the time goes in v3:
time: 139 us
  Pallas kernels  137 us (99%)
    pallas_call x1, Pallas kernels, on_device(): pl.pallas_call(functools.partial(kernel, (n_grp, shard, height, breadth))...  131 us
    pallas_call x1, Pallas kernels, finish(): pl.pallas_call(finish_kernel, out_shape=(jax.ShapeDtypeStruct((n_grp, sha...  6.31 us

profile of v3, /device:TPU:1, one launch (start us, length us, event | category | flops | bytes accessed | tf_op | source)
XLA Modules:
  0.0 138.5 jit_solution(18022749167281043953)
XLA Ops:
  0.6 131.0 %up_backward.1 = (bf16[512,1408]{1,0:T(8,128)(2,1)}, bf16[1280,2048]{1,0:T(8,128)(2,1)}, f32[10,16]{1,0:T(8,128)}) custom-call(s32[8,8]{1,0:T(8,128)} %counts.1, bf16[128,64]{1,0:T(8,128)(2,1)} %bitcast.17, bf16[128,8192]{1,0:T(8,128)(2,1)} %bitcast.14, bf16[128,5120]{1,0:T(8,128)(2,1)} %bitcast.16, bf16[1280,2048]{1,0:T(8,128)(2,1)} %bitcast.13), custom_call_target="tpu_custom_call" | custom-call | tf_op jit(solution)/shard_map/up_backward/pallas_call | solution.py:446
  131.6 0.0 copy-start
  131.6 6.3 %finish.1 = (bf16[8,16,5120]{2,1,0:T(8,128)(2,1)}, bf16[8,16,40]{2,1,0:T(8,128)(2,1)}, bf16[1280,2048]{1,0:T(8,128)(2,1)}) custom-call(bf16[8,4,16,1408]{3,2,1,0:T(8,128)(2,1)} %bitcast.15, bf16[1280,2048]{1,0:T(8,128)(2,1)} %get-tuple-element.11.dw), custom_call_target="tpu_custom_call" | custom-call | tf_op jit(solution)/shard_map/finish/pallas_call | solution.py:554
  137.9 0.0 copy-done
  137.9 0.6 copy.11
Async XLA Ops:
  131.6 6.3 %copy-start = (f32[10,16]{1,0:T(8,128)S(1)}, f32[10,16]{1,0:T(8,128)}, u32[]{:S(2)}) copy-start(f32[10,16]{1,0:T(8,128)} %get-tuple-element.15) | copy-start | bytes 1924

commit v4 on v3

--- a/solution.py
+++ b/solution.py
@@ -145,7 +145,7 @@
         return (y + d + SIDE) % SIDE
 
     x_order = []
-    for near in range(1, nx // 2 + 1):
+    for near in range(nx // 2, 0, -1):
         for dc in range(2):
             x_order.append((near, dc))
             if nx - near != near:

time: 139 us -> 139 us (level)
  no operation moved by 1% of the time
where the time goes in v4:
time: 139 us; the launch traced here: 138 us
  Pallas kernels  137 us (99%)
    pallas_call x1, Pallas kernels, on_device(): pl.pallas_call(functools.partial(kernel, (n_grp, shard, height, breadth))...  131 us
    pallas_call x1, Pallas kernels, finish(): pl.pallas_call(finish_kernel, out_shape=(jax.ShapeDtypeStruct((n_grp, sha...  6.31 us

profile of v4, /device:TPU:1, one launch (start us, length us, event | category | flops | bytes accessed | tf_op | source)
XLA Modules:
  0.0 138.2 jit_solution(4255935991690800112)
XLA Ops:
  0.6 130.7 %up_backward.1 = (bf16[512,1408]{1,0:T(8,128)(2,1)}, bf16[1280,2048]{1,0:T(8,128)(2,1)}, f32[10,16]{1,0:T(8,128)}) custom-call(s32[8,8]{1,0:T(8,128)} %counts.1, bf16[128,64]{1,0:T(8,128)(2,1)} %bitcast.17, bf16[128,8192]{1,0:T(8,128)(2,1)} %bitcast.14, bf16[128,5120]{1,0:T(8,128)(2,1)} %bitcast.16, bf16[1280,2048]{1,0:T(8,128)(2,1)} %bitcast.13), custom_call_target="tpu_custom_call" | custom-call | tf_op jit(solution)/shard_map/up_backward/pallas_call | solution.py:446
  131.3 0.0 copy-start
  131.3 6.3 %finish.1 = (bf16[8,16,5120]{2,1,0:T(8,128)(2,1)}, bf16[8,16,40]{2,1,0:T(8,128)(2,1)}, bf16[1280,2048]{1,0:T(8,128)(2,1)}) custom-call(bf16[8,4,16,1408]{3,2,1,0:T(8,128)(2,1)} %bitcast.15, bf16[1280,2048]{1,0:T(8,128)(2,1)} %get-tuple-element.11.dw), custom_call_target="tpu_custom_call" | custom-call | tf_op jit(solution)/shard_map/finish/pallas_call | solution.py:554
  137.6 0.0 copy-done
  137.6 0.6 copy.11
Async XLA Ops:
  131.3 6.3 %copy-start = (f32[10,16]{1,0:T(8,128)S(1)}, f32[10,16]{1,0:T(8,128)}, u32[]{:S(2)}) copy-start(f32[10,16]{1,0:T(8,128)} %get-tuple-element.15) | copy-start | bytes 1924
